TPU v7x, 32 devices: a whole 2x2x4 slice. The times are simulated.
32 devices in a mesh: groups: 2 (over y), row: 8 (over z, x), col: 2 (over core).
Axes of the slice: x: 2, y: 2, z: 4, core: 2. Of those that a mesh axis runs over, the one named last changes fastest.
Arguments:
- inputs: bfloat16 [1024, 8192], P(('groups', 'row'), 'col'), parts along dimension 0, may hold values from -6 to 6
- gate_saved: bfloat16 [1024, 16384], P(('groups', 'col'), 'row'), parts along dimension 0, may hold values from -8 to 8
- up_saved: bfloat16 [1024, 16384], P(('groups', 'col'), 'row'), parts along dimension 0, may hold values from -6 to 6
- cotangent: bfloat16 [1024, 8192], P(('groups', 'row'), 'col'), parts along dimension 0, may hold values from -2 to 2
- gate_weight: bfloat16 [8192, 16384], P('col', 'row'), may hold values from -0.0625 to 0.0625
- up_weight: bfloat16 [8192, 16384], P('col', 'row'), may hold values from -0.0625 to 0.0625
- down_weight: bfloat16 [16384, 8192], P('row', 'col'), may hold values from -0.046875 to 0.046875
Outputs:
- grad_inputs: bfloat16 [1024, 8192], P(('groups', 'row'), 'col'), parts along dimension 0
- grad_gate: bfloat16 [16384, 16384], P(('groups', 'col'), 'row'), parts along dimension 0
- grad_up: bfloat16 [16384, 16384], P(('groups', 'col'), 'row'), parts along dimension 0
- grad_down: bfloat16 [32768, 8192], P(('groups', 'row'), 'col'), parts along dimension 0
There are 2 independent parts, one for each index of `groups`. A program takes and returns all parts, laid end to end along the dimension named above; an argument that names none is the same for every part. Nothing has to cross between parts.
All inputs are finite; a program needn't handle non-finite values.
Results may differ from a plain program's by a relative error of at most 0.0051.
Values may be sent and summed in bfloat16 or wider, within the bound.
A program may use at most 256 MiB of HBM per device.

v0:
```python
import jax
import jax.numpy as jnp
from jax import lax
from jax.sharding import PartitionSpec as P


def swiglu_back(gate_vals, up_vals, grad_hidden):
    gvals = gate_vals.astype(jnp.float32)
    uvals = up_vals.astype(jnp.float32)
    sigma = jax.nn.sigmoid(gvals)
    hidden = (gvals * sigma * uvals).astype(jnp.bfloat16)
    grad_gate_act = (grad_hidden * uvals * sigma * (1.0 + gvals * (1.0 - sigma))).astype(
        jnp.bfloat16
    )
    grad_up_act = (grad_hidden * gvals * sigma).astype(jnp.bfloat16)
    return (hidden, grad_gate_act, grad_up_act)


def per_device(inputs, gate_saved, up_saved, cotangent, gate_weight, up_weight, down_weight):
    contract_rows = (((0,), (0,)), ((), ()))
    contract_cols = (((1,), (1,)), ((), ()))
    cotan_all = lax.all_gather(cotangent, "row", axis=0, tiled=True)
    partial_hidden = lax.dot_general(
        cotan_all, down_weight, contract_cols, preferred_element_type=jnp.float32
    )
    gates_all, ups_all = (
        lax.all_gather(gate_saved, "col", axis=0, tiled=True),
        lax.all_gather(up_saved, "col", axis=0, tiled=True),
    )
    summed = lax.psum(partial_hidden, "col")
    hidden, grad_g, grad_u = swiglu_back(gates_all, ups_all, summed)
    grad_down = lax.dot_general(
        hidden, cotan_all, contract_rows, preferred_element_type=jnp.float32
    ).astype(jnp.bfloat16)
    inputs_all = lax.all_gather(inputs, "row", axis=0, tiled=True)
    grad_gate = lax.dot_general(
        inputs_all, grad_g, contract_rows, preferred_element_type=jnp.float32
    ).astype(jnp.bfloat16)
    grad_up = lax.dot_general(
        inputs_all, grad_u, contract_rows, preferred_element_type=jnp.float32
    ).astype(jnp.bfloat16)
    total = lax.dot_general(grad_g, gate_weight, contract_cols, preferred_element_type=jnp.float32)
    grad_inputs = lax.psum_scatter(
        total
        + lax.dot_general(grad_u, up_weight, contract_cols, preferred_element_type=jnp.float32),
        "row",
        scatter_dimension=0,
        tiled=True,
    ).astype(jnp.bfloat16)
    return (grad_inputs, grad_gate, grad_up, grad_down)


def solution(mesh):
    return jax.shard_map(
        per_device,
        mesh=mesh,
        in_specs=(
            P(("groups", "row"), "col"),
            P(("groups", "col"), "row"),
            P(("groups", "col"), "row"),
            P(("groups", "row"), "col"),
            P("col", "row"),
            P("col", "row"),
            P("row", "col"),
        ),
        out_specs=(
            P(("groups", "row"), "col"),
            P(("groups", "col"), "row"),
            P(("groups", "col"), "row"),
            P(("groups", "row"), "col"),
        ),
        check_vma=False,
    )
```

profile of v0, /device:TPU:17, one launch (start us, length us, event | category | flops | bytes accessed | tf_op | source)
XLA Modules:
  0.0 376.8 jit_solution(7625424705951463349)
XLA Ops:
  7.2 0.0 all-gather.5.cloned.1.call-start
  7.2 0.7 all-gather.5.cloned.1.call-update
  7.9 0.0 all-gather.9.cloned.1.call-start
  7.9 0.7 all-gather.9.cloned.1.call-update
  8.6 0.0 all-gather.7.cloned.1.call-start
  8.7 0.7 all-gather.7.cloned.1.call-update
  9.4 0.0 all-reduce.2.cloned.1.call-start
  9.4 74.0 %all-gather.5.cloned.1.call-done = bf16[512,4096]{1,0:T(8,128)(2,1)} async-done(((bf16[64,4096]{1,0:T(8,128)(2,1)}), bf16[512,4096]{1,0:T(8,128)(2,1)}) %all-gather.5.cloned.1.call-update) | async-done | bytes 4194320 | tf_op jit(solution)/shard_map/all_gather | solution.py:22
  83.4 15.0 %fusion.15 = f32[512,2048]{1,0:T(8,128)} fusion(bf16[512,4096]{1,0:T(8,128)(2,1)} %all-gather.5.cloned.1.call-done, bf16[2048,4096]{1,0:T(8,128)(2,1)} %param.13), kind=kOutput, calls=%fused_computation.22 | convolution fusion | flops 8589934592 | bytes 25165824 | tf_op jit(solution)/shard_map/dot_general | solution.py:23
  98.4 0.0 all-reduce.2.cloned.1.call-update
  98.4 0.0 all-gather.11.cloned.1.call-start
  98.4 0.5 all-gather.11.cloned.1.call-update
  99.0 0.2 reduce-scatter.2.cloned.1.call-start
  99.2 0.0 all-gather.9.cloned.1.call-done
  99.2 9.9 %all-gather.7.cloned.1.call-done = bf16[512,2048]{1,0:T(8,128)(2,1)} async-done(((bf16[256,2048]{1,0:T(8,128)(2,1)}), bf16[512,2048]{1,0:T(8,128)(2,1)}) %all-gather.7.cloned.1.call-update) | async-done | bytes 2097168 | tf_op jit(solution)/shard_map/all_gather | solution.py:28
  109.1 32.5 %all-reduce.2.cloned.1.call-done = f32[512,2048]{1,0:T(8,128)} async-done(((f32[512,2048]{1,0:T(8,128)}), f32[512,2048]{1,0:T(8,128)}) %all-reduce.2.cloned.1.call-update) | async-done | bytes 4194320 | tf_op jit(solution)/shard_map/psum | solution.py:30
  141.6 5.2 %fusion.2 = bf16[512,2048]{1,0:T(8,128)(2,1)S(1)} fusion(f32[512,2048]{1,0:T(8,128)} %all-reduce.2.cloned.1.call-done, bf16[512,2048]{1,0:T(8,128)(2,1)} %all-gather.7.cloned.1.call-done, bf16[512,2048]{1,0:T(8,128)(2,1)} %all-gather.9.cloned.1.call-done), kind=kLoop, calls=%fused_computation.12 | loop fusion | flops 12582912 | bytes 10485760 | tf_op jit(solution)/shard_map/convert_element_type | solution.py:12
  146.9 0.0 copy-start.1
  146.9 1.3 copy-done.1
  148.2 0.0 copy-start
  148.2 14.6 %fusion.16 = f32[512,4096]{1,0:T(8,128)} fusion(bf16[512,2048]{1,0:T(8,128)(2,1)S(1)} %fusion.2, bf16[4096,2048]{1,0:T(8,128)(2,1)} %param.11), kind=kOutput, calls=%fused_computation.23 | convolution fusion | flops 8589934592 | bytes 27262976 | tf_op jit(solution)/shard_map/dot_general | solution.py:42
  162.8 0.0 copy-done
  162.8 17.2 %convolution_add_fusion = f32[512,4096]{1,0:T(8,128)} fusion(f32[512,4096]{1,0:T(8,128)} %fusion.16, bf16[4096,2048]{1,0:T(8,128)(2,1)} %param.12, f32[512,2048]{1,0:T(8,128)} %all-reduce.2.cloned.1.call-done, bf16[512,2048]{1,0:T(8,128)(2,1)S(1)} %copy-done), kind=kOutput, calls=%fused_computation.7 | convolution fusion | flops 8599371776 | bytes 39845888 | tf_op jit(solution)/shard_map/dot_general | solution.py:45
  180.0 0.0 reduce-scatter.2.cloned.1.call-update
  180.1 15.6 %convolution_convert_fusion = bf16[2048,4096]{1,0:T(8,128)(2,1)} fusion(bf16[512,4096]{1,0:T(8,128)(2,1)} %all-gather.5.cloned.1.call-done, bf16[512,2048]{1,0:T(8,128)(2,1)} %all-gather.7.cloned.1.call-done, bf16[512,2048]{1,0:T(8,128)(2,1)S(1)} %copy-done), kind=kOutput, calls=%fused_computation.2 | convolution fusion | flops 8606711808 | bytes 25165824 | tf_op jit(solution)/shard_map/dot_general | solution.py:32
  195.7 20.8 %all-gather.11.cloned.1.call-done = bf16[512,4096]{1,0:T(8,128)(2,1)} async-done(((bf16[64,4096]{1,0:T(8,128)(2,1)}), bf16[512,4096]{1,0:T(8,128)(2,1)}) %all-gather.11.cloned.1.call-update) | async-done | bytes 4194320 | tf_op jit(solution)/shard_map/all_gather | solution.py:35
  216.5 15.1 %convert_bitcast_fusion.1 = bf16[4096,2048]{0,1:T(8,128)(2,1)} fusion(bf16[512,2048]{1,0:T(8,128)(2,1)} %copy-done.1, bf16[512,4096]{1,0:T(8,128)(2,1)} %all-gather.11.cloned.1.call-done), kind=kOutput, calls=%fused_computation.1 | convolution fusion | flops 8598323200 | bytes 23068672 | tf_op jit(solution)/shard_map/dot_general | solution.py:36
  231.5 22.5 %copy.11 = bf16[4096,2048]{1,0:T(8,128)(2,1)} copy(bf16[4096,2048]{0,1:T(8,128)(2,1)} %convert_bitcast_fusion.1) | data formatting | bytes 33554432
  254.0 15.6 %convert_bitcast_fusion = bf16[4096,2048]{0,1:T(8,128)(2,1)} fusion(bf16[512,4096]{1,0:T(8,128)(2,1)} %all-gather.11.cloned.1.call-done, f32[512,2048]{1,0:T(8,128)} %all-reduce.2.cloned.1.call-done, bf16[512,2048]{1,0:T(8,128)(2,1)S(1)} %copy-done), kind=kOutput, calls=%fused_computation | convolution fusion | flops 8605663232 | bytes 27262976 | tf_op jit(solution)/shard_map/dot_general | solution.py:39
  269.6 22.5 %copy.12 = bf16[4096,2048]{1,0:T(8,128)(2,1)} copy(bf16[4096,2048]{0,1:T(8,128)(2,1)} %convert_bitcast_fusion) | data formatting | bytes 33554432
  292.1 75.8 %reduce-scatter.2.cloned.1.call-done = f32[64,4096]{1,0:T(8,128)} async-done(((f32[512,4096]{1,0:T(8,128)}), f32[64,4096]{1,0:T(8,128)}) %reduce-scatter.2.cloned.1.call-update) | async-done | bytes 1048592 | tf_op jit(solution)/shard_map/reduce_scatter | solution.py:43
  367.9 2.1 convert_element_type.37
Async XLA Ops:
  7.2 76.2 %all-gather.5.cloned.1.call-start = ((), (), s32[]{:S(2)}) async-start(), calls=%async_computation.1 | async-start | bytes 4718592 | tf_op jit(solution)/shard_map/all_gather | solution.py:22
  7.9 91.3 %all-gather.9.cloned.1.call-start = ((), (), s32[]{:S(2)}) async-start(), calls=%async_computation.4 | async-start | bytes 3145728 | tf_op jit(solution)/shard_map/all_gather | solution.py:27
  8.6 100.5 %all-gather.7.cloned.1.call-start = ((), (), s32[]{:S(2)}) async-start(), calls=%async_computation.3 | async-start | bytes 3145728 | tf_op jit(solution)/shard_map/all_gather | solution.py:28
  9.4 132.3 %all-reduce.2.cloned.1.call-start = ((), (), s32[]{:S(2)}) async-start(), calls=%async_computation.2 | async-start | bytes 8388608 | tf_op jit(solution)/shard_map/psum | solution.py:30
  98.4 118.1 %all-gather.11.cloned.1.call-start = ((), (), s32[]{:S(2)}) async-start(), calls=%async_computation.6 | async-start | bytes 4718592 | tf_op jit(solution)/shard_map/all_gather | solution.py:35
  99.0 268.9 %reduce-scatter.2.cloned.1.call-start = ((), (), s32[]{:S(2)}) async-start(), calls=%async_computation.5 | async-start | bytes 9437184 | tf_op jit(solution)/shard_map/reduce_scatter | solution.py:43
  146.9 1.3 copy-start.1
  148.2 14.6 %copy-start = (bf16[512,2048]{1,0:T(8,128)(2,1)S(1)}, bf16[512,2048]{1,0:T(8,128)(2,1)}, u32[]{:S(2)}) copy-start(bf16[512,2048]{1,0:T(8,128)(2,1)} %all-gather.9.cloned.1.call-done) | copy-start | bytes 6291460
Sparse Core Ops, SparseCore 0:
  10.1 73.2 all-gather.4
  84.9 10.7 all-gather.8
  97.3 11.7 all-gather.6
  112.0 29.5 all-reduce.1
  143.8 72.6 all-gather.10
  220.4 147.4 reduce-scatter.1
where the time goes:
time: 381 us; the launch traced here: 377 us
  waiting for transfers between devices  216 us (57%)
  matrix products  93 us (24%)
  local copies, waits for them, and re-layouts  46.3 us (12%)
  between operations  14.1 us (4%)
  other arithmetic  7.31 us (2%)
    reduce_scatter x1, waiting for transfers between devices, per_device(): lax.psum_scatter(total + lax.dot_general(grad_u, up_weight, contract_cols...  75.8 us
    all_gather x1, waiting for transfers between devices, per_device(): cotan_all = lax.all_gather(cotangent, 'row', axis=0, tiled=True)  74 us
    unnamed x6, local copies, waits for them, and re-layouts  46.3 us
    psum x1, waiting for transfers between devices, per_device(): summed = lax.psum(partial_hidden, 'col')  32.5 us
    all_gather x1, waiting for transfers between devices, per_device(): inputs_all = lax.all_gather(inputs, 'row', axis=0, tiled=True)  20.8 us
    dot_general x1, matrix products, per_device(): lax.dot_general(grad_u, up_weight, contract_cols, preferred_element_type=...  17.2 us
    dot_general x1, matrix products, per_device(): lax.dot_general(hidden, cotan_all, contract_rows, preferred_element_type=...  15.6 us
    dot_general x1, matrix products, per_device(): lax.dot_general(inputs_all, grad_u, contract_rows, preferred_element_type...  15.6 us
  transfers between devices with their start and end apart: 6, of which 5 were waited for; matrix products, arithmetic and copies ran while one was open for 38% of the time, Pallas kernels for 0%

commit v1 on v0

v1 whole, which is shorter than its diff:
```python
import jax
import jax.numpy as jnp
from jax import lax
from jax.experimental import pallas as pl
from jax.experimental.pallas import tpu as pltpu
from jax.sharding import PartitionSpec as P

ROWS = (((0,), (0,)), ((), ()))
COLS = (((1,), (1,)), ((), ()))


def swiglu_back(gate_vals, up_vals, grad_hidden):
    gvals = gate_vals.astype(jnp.float32)
    uvals = up_vals.astype(jnp.float32)
    sigma = jax.nn.sigmoid(gvals)
    hidden = (gvals * sigma * uvals).astype(jnp.bfloat16)
    grad_gate_act = (grad_hidden * uvals * sigma * (1.0 + gvals * (1.0 - sigma))).astype(
        jnp.bfloat16
    )
    grad_up_act = (grad_hidden * gvals * sigma).astype(jnp.bfloat16)
    return (hidden, grad_gate_act, grad_up_act)


def weight_grads_kernel(n_right, left_ref, *refs):
    left = left_ref[...].T
    for right_ref, out_ref in zip(refs[:n_right], refs[n_right:]):
        out_ref[...] = jnp.dot(
            left, right_ref[...], preferred_element_type=jnp.float32
        ).astype(jnp.bfloat16)


def weight_grads(left, rights, blocks):
    tokens, m = left.shape
    bm = m // blocks
    kern = lambda *refs: weight_grads_kernel(len(rights), *refs)
    n = rights[0].shape[1]
    return pl.pallas_call(
        kern,
        grid=(blocks,),
        in_specs=[pl.BlockSpec((tokens, bm), lambda i: (0, i))]
        + [pl.BlockSpec((tokens, n), lambda i: (0, 0)) for _ in rights],
        out_specs=[pl.BlockSpec((bm, n), lambda i: (i, 0)) for _ in rights],
        out_shape=[jax.ShapeDtypeStruct((m, n), jnp.bfloat16) for _ in rights],
        cost_estimate=pl.CostEstimate(
            flops=2 * tokens * m * n * len(rights),
            bytes_accessed=2 * (tokens * m + (tokens * n + m * n) * len(rights)),
            transcendentals=0,
        ),
        compiler_params=pltpu.CompilerParams(vmem_limit_bytes=56 * 2**20),
    )(left, *rights)


def per_device(inputs, gate_saved, up_saved, cotangent, gate_weight, up_weight, down_weight):
    cotan_all = lax.all_gather(cotangent, "row", axis=0, tiled=True)
    partial_hidden = lax.dot_general(
        cotan_all, down_weight, COLS, preferred_element_type=jnp.float32
    )
    gates_all, ups_all = (
        lax.all_gather(gate_saved, "col", axis=0, tiled=True),
        lax.all_gather(up_saved, "col", axis=0, tiled=True),
    )
    summed = lax.psum(partial_hidden, "col")
    hidden, grad_g, grad_u = swiglu_back(gates_all, ups_all, summed)
    total = lax.dot_general(grad_g, gate_weight, COLS, preferred_element_type=jnp.float32)
    total = total + lax.dot_general(grad_u, up_weight, COLS, preferred_element_type=jnp.float32)
    grad_inputs = lax.psum_scatter(total, "row", scatter_dimension=0, tiled=True).astype(
        jnp.bfloat16
    )
    inputs_all = lax.all_gather(inputs, "row", axis=0, tiled=True)
    (grad_down,) = weight_grads(hidden, (cotan_all,), max(1, hidden.shape[1] // 256))
    grad_gate, grad_up = weight_grads(inputs_all, (grad_g, grad_u), 8)
    return (grad_inputs, grad_gate, grad_up, grad_down)


def solution(mesh):
    return jax.shard_map(
        per_device,
        mesh=mesh,
        in_specs=(
            P(("groups", "row"), "col"),
            P(("groups", "col"), "row"),
            P(("groups", "col"), "row"),
            P(("groups", "row"), "col"),
            P("col", "row"),
            P("col", "row"),
            P("row", "col"),
        ),
        out_specs=(
            P(("groups", "row"), "col"),
            P(("groups", "col"), "row"),
            P(("groups", "col"), "row"),
            P(("groups", "row"), "col"),
        ),
        check_vma=False,
    )
```

time: 381 us -> 380 us (level)
  waiting for transfers between devices: 216 us -> 271 us
  matrix products: 93 us -> 46.7 us
  local copies, waits for them, and re-layouts: 46.3 us -> 0.01 us
  Pallas kernels: 0 us -> 37 us
    reduce_scatter x1, waiting for transfers between devices: 75.8 us -> 129 us  [per_device(): lax.psum_scatter(total, 'row', scatter_dimension=0, tiled=True)]
    dot_general x6 -> x3, matrix products: 93 us -> 46.7 us  [the longest x1 16 us: per_device(): lax.dot_general(grad_g, gate_weight, COLS, preferred_element_type=jnp.flo...]
    unnamed x6 -> x4, local copies, waits for them, and re-layouts: 46.3 us -> 0.01 us
    pallas_call x0 -> x2, Pallas kernels: none -> 37 us  [weight_grads(): pl.pallas_call(kern, grid=(blocks,), in_specs=[pl.BlockSpec((tokens, bm),...]
    all_gather x1, waiting for transfers between devices: 9.88 us -> 0.02 us  [per_device(): lax.all_gather(up_saved, 'col', axis=0, tiled=True)]
    all_gather x1, waiting for transfers between devices: 0.02 us -> 9.88 us  [per_device(): lax.all_gather(gate_saved, 'col', axis=0, tiled=True)]
  transfers between devices with their start and end apart: 6 -> 6, of which waited for: 5 -> 5; matrix products, arithmetic and copies ran while one was open for 38% -> 14% of each run, Pallas kernels for 0% -> 10%
where the time goes in v1:
time: 380 us; the launch traced here: 377 us
  waiting for transfers between devices  271 us (71%)
  matrix products  46.7 us (12%)
  Pallas kernels  37 us (10%)
  between operations  14.1 us (4%)
  other arithmetic  7.73 us (2%)
    reduce_scatter x1, waiting for transfers between devices, per_device(): lax.psum_scatter(total, 'row', scatter_dimension=0, tiled=True)  129 us
    all_gather x1, waiting for transfers between devices, per_device(): cotan_all = lax.all_gather(cotangent, 'row', axis=0, tiled=True)  74 us
    pallas_call x2, Pallas kernels, weight_grads(): pl.pallas_call(kern, grid=(blocks,), in_specs=[pl.BlockSpec((tokens, bm),...  37 us
    psum x1, waiting for transfers between devices, per_device(): summed = lax.psum(partial_hidden, 'col')  32.5 us
    all_gather x1, waiting for transfers between devices, per_device(): inputs_all = lax.all_gather(inputs, 'row', axis=0, tiled=True)  23.4 us
    dot_general x1, matrix products, per_device(): lax.dot_general(grad_g, gate_weight, COLS, preferred_element_type=jnp.flo...  16 us
    dot_general x1, matrix products, per_device(): lax.dot_general(grad_u, up_weight, COLS, preferred_element_type=jnp.float32)  15.7 us
    dot_general x1, matrix products, per_device(): lax.dot_general(cotan_all, down_weight, COLS, preferred_element_type=jnp....  15 us
  transfers between devices with their start and end apart: 6, of which 5 were waited for; matrix products, arithmetic and copies ran while one was open for 14% of the time, Pallas kernels for 10%

profile of v1, /device:TPU:17, one launch (start us, length us, event | category | flops | bytes accessed | tf_op | source)
XLA Modules:
  0.0 376.8 jit_solution(13282244871516558594)
XLA Ops:
  7.2 0.0 all-gather.5.cloned.1.call-start
  7.2 0.7 all-gather.5.cloned.1.call-update
  7.9 0.0 all-gather.7.cloned.1.call-start
  7.9 0.7 all-gather.7.cloned.1.call-update
  8.6 0.0 all-gather.9.cloned.1.call-start
  8.7 0.7 all-gather.9.cloned.1.call-update
  9.4 0.0 all-reduce.2.cloned.1.call-start
  9.4 74.0 %all-gather.5.cloned.1.call-done.refs_1_ = bf16[512,4096]{1,0:T(8,128)(2,1)} async-done(((bf16[64,4096]{1,0:T(8,128)(2,1)}), bf16[512,4096]{1,0:T(8,128)(2,1)}) %all-gather.5.cloned.1.call-update) | async-done | bytes 4194320 | tf_op jit(solution)/shard_map/all_gather | solution.py:54
  83.4 15.0 %fusion.10 = f32[512,2048]{1,0:T(8,128)} fusion(bf16[512,4096]{1,0:T(8,128)(2,1)} %all-gather.5.cloned.1.call-done.refs_1_, bf16[2048,4096]{1,0:T(8,128)(2,1)} %param.13), kind=kOutput, calls=%fused_computation.17 | convolution fusion | flops 8589934592 | bytes 25165824 | tf_op jit(solution)/shard_map/dot_general | solution.py:55
  98.4 0.0 all-reduce.2.cloned.1.call-update
  98.4 0.0 all-gather.11.cloned.1.call-start
  98.4 0.5 all-gather.11.cloned.1.call-update
  99.0 0.2 reduce-scatter.2.cloned.1.call-start
  99.2 0.0 all-gather.7.cloned.1.call-done
  99.2 9.9 %all-gather.9.cloned.1.call-done = bf16[512,2048]{1,0:T(8,128)(2,1)} async-done(((bf16[256,2048]{1,0:T(8,128)(2,1)}), bf16[512,2048]{1,0:T(8,128)(2,1)}) %all-gather.9.cloned.1.call-update) | async-done | bytes 2097168 | tf_op jit(solution)/shard_map/all_gather | solution.py:59
  109.1 32.5 %all-reduce.2.cloned.1.call-done = f32[512,2048]{1,0:T(8,128)} async-done(((f32[512,2048]{1,0:T(8,128)}), f32[512,2048]{1,0:T(8,128)}) %all-reduce.2.cloned.1.call-update) | async-done | bytes 4194320 | tf_op jit(solution)/shard_map/psum | solution.py:62
  141.6 5.7 %fusion.9 = (bf16[512,2048]{1,0:T(8,128)(2,1)S(1)}, bf16[512,2048]{1,0:T(8,128)(2,1)S(1)}, bf16[512,2048]{1,0:T(8,128)(2,1)}) fusion(f32[512,2048]{1,0:T(8,128)} %all-reduce.2.cloned.1.call-done, bf16[512,2048]{1,0:T(8,128)(2,1)} %all-gather.9.cloned.1.call-done, bf16[512,2048]{1,0:T(8,128)(2,1)} %all-gather.7.cloned.1.call-done), kind=kLoop, calls=%fused_computation.16 | loop fusion | flops 18874368 | bytes 14680064 | tf_op jit(solution)/shard_map/convert_element_type | solution.py:20
  147.3 0.0 copy-start.1
  147.3 0.0 copy-start
  147.3 16.0 %fusion.11 = f32[512,4096]{1,0:T(8,128)} fusion(bf16[512,2048]{1,0:T(8,128)(2,1)S(1)} %get-tuple-element.9.refs_1_, bf16[4096,2048]{1,0:T(8,128)(2,1)} %param.11), kind=kOutput, calls=%fused_computation.18 | convolution fusion | flops 8589934592 | bytes 27262976 | tf_op jit(solution)/shard_map/dot_general | solution.py:64
  163.3 0.0 copy-done.1
  163.3 0.0 copy-done
  163.3 15.7 %convolution_add_fusion = f32[512,4096]{1,0:T(8,128)} fusion(f32[512,4096]{1,0:T(8,128)} %fusion.11, bf16[512,2048]{1,0:T(8,128)(2,1)S(1)} %get-tuple-element.8.refs_2_, bf16[4096,2048]{1,0:T(8,128)(2,1)} %param.12), kind=kOutput, calls=%fused_computation.4 | convolution fusion | flops 8592031744 | bytes 35651584 | tf_op jit(solution)/shard_map/dot_general | solution.py:65
  179.0 0.0 reduce-scatter.2.cloned.1.call-update
  179.1 14.0 %shard_map.103 = bf16[2048,4096]{1,0:T(8,128)(2,1)} custom-call(bf16[512,2048]{1,0:T(8,128)(2,1)} %get-tuple-element.10.refs_0_, bf16[512,4096]{1,0:T(8,128)(2,1)} %all-gather.5.cloned.1.call-done.refs_1_), custom_call_target="tpu_custom_call" | custom-call | flops 8589934592 | bytes 23068672 | tf_op jit(solution)/shard_map/pallas_call | solution.py:37
  193.1 23.4 %all-gather.11.cloned.1.call-done.refs_0_ = bf16[512,4096]{1,0:T(8,128)(2,1)} async-done(((bf16[64,4096]{1,0:T(8,128)(2,1)}), bf16[512,4096]{1,0:T(8,128)(2,1)}) %all-gather.11.cloned.1.call-update) | async-done | bytes 4194320 | tf_op jit(solution)/shard_map/all_gather | solution.py:69
  216.5 22.9 %shard_map.102 = (bf16[4096,2048]{1,0:T(8,128)(2,1)}, bf16[4096,2048]{1,0:T(8,128)(2,1)}) custom-call(bf16[512,4096]{1,0:T(8,128)(2,1)} %all-gather.11.cloned.1.call-done.refs_0_, bf16[512,2048]{1,0:T(8,128)(2,1)} %copy-done.1, bf16[512,2048]{1,0:T(8,128)(2,1)} %copy-done), custom_call_target="tpu_custom_call" | custom-call | flops 17179869184 | bytes 41943040 | tf_op jit(solution)/shard_map/pallas_call | solution.py:37
  239.4 128.5 %reduce-scatter.2.cloned.1.call-done = f32[64,4096]{1,0:T(8,128)} async-done(((f32[512,4096]{1,0:T(8,128)}), f32[64,4096]{1,0:T(8,128)}) %reduce-scatter.2.cloned.1.call-update) | async-done | bytes 1048592 | tf_op jit(solution)/shard_map/reduce_scatter | solution.py:66
  367.9 2.1 convert_element_type.22
Async XLA Ops:
  7.2 76.2 %all-gather.5.cloned.1.call-start = ((), (), s32[]{:S(2)}) async-start(), calls=%async_computation.1 | async-start | bytes 4718592 | tf_op jit(solution)/shard_map/all_gather | solution.py:54
  7.9 91.3 %all-gather.7.cloned.1.call-start = ((), (), s32[]{:S(2)}) async-start(), calls=%async_computation.3 | async-start | bytes 3145728 | tf_op jit(solution)/shard_map/all_gather | solution.py:60
  8.6 100.5 %all-gather.9.cloned.1.call-start = ((), (), s32[]{:S(2)}) async-start(), calls=%async_computation.4 | async-start | bytes 3145728 | tf_op jit(solution)/shard_map/all_gather | solution.py:59
  9.4 132.3 %all-reduce.2.cloned.1.call-start = ((), (), s32[]{:S(2)}) async-start(), calls=%async_computation.2 | async-start | bytes 8388608 | tf_op jit(solution)/shard_map/psum | solution.py:62
  98.4 118.1 %all-gather.11.cloned.1.call-start = ((), (), s32[]{:S(2)}) async-start(), calls=%async_computation.6 | async-start | bytes 4718592 | tf_op jit(solution)/shard_map/all_gather | solution.py:69
  99.0 268.9 %reduce-scatter.2.cloned.1.call-start = ((), (), s32[]{:S(2)}) async-start(), calls=%async_computation.5 | async-start | bytes 9437184 | tf_op jit(solution)/shard_map/reduce_scatter | solution.py:66
  147.3 16.0 %copy-start.1 = (bf16[512,2048]{1,0:T(8,128)(2,1)}, bf16[512,2048]{1,0:T(8,128)(2,1)S(1)}, u32[]{:S(2)}) copy-start(bf16[512,2048]{1,0:T(8,128)(2,1)S(1)} %get-tuple-element.9.refs_1_) | copy-start | bytes 6291460
  147.3 16.0 %copy-start = (bf16[512,2048]{1,0:T(8,128)(2,1)}, bf16[512,2048]{1,0:T(8,128)(2,1)S(1)}, u32[]{:S(2)}) copy-start(bf16[512,2048]{1,0:T(8,128)(2,1)S(1)} %get-tuple-element.8.refs_2_) | copy-start | bytes 6291460
Sparse Core Ops, SparseCore 0:
  10.1 73.2 all-gather.4
  84.9 10.7 all-gather.6
  97.3 11.7 all-gather.8
  112.0 29.5 all-reduce.1
  143.8 72.6 all-gather.10
  220.4 147.4 reduce-scatter.1

commit v2 on v1

--- a/solution.py
+++ b/solution.py
@@ -1,3 +1,5 @@
+import functools
+
 import jax
 import jax.numpy as jnp
 from jax import lax
@@ -50,7 +52,7 @@
     )(left, *rights)
 
 
-def per_device(inputs, gate_saved, up_saved, cotangent, gate_weight, up_weight, down_weight):
+def plain(inputs, gate_saved, up_saved, cotangent, gate_weight, up_weight, down_weight):
     cotan_all = lax.all_gather(cotangent, "row", axis=0, tiled=True)
     partial_hidden = lax.dot_general(
         cotan_all, down_weight, COLS, preferred_element_type=jnp.float32
@@ -72,6 +74,364 @@
     return (grad_inputs, grad_gate, grad_up, grad_down)
 
 
+MESH = pl.DeviceIdType.MESH
+
+
+def lines_of(rows):
+    across = 1
+    while (2 * across) ** 3 <= rows:
+        across *= 2
+    return rows // across, across
+
+
+class Place:
+    def __init__(self, rows):
+        self.deep, self.across = lines_of(rows)
+        self.me = lax.axis_index("row")
+        self.z, self.x = self.me // self.across, lax.rem(self.me, self.across)
+
+    def z_at(self, d):
+        return lax.rem(self.z + d + self.deep, self.deep)
+
+    def x_at(self, e):
+        return lax.rem(self.x + e + self.across, self.across)
+
+    def row(self, z, x):
+        return z * self.across + x
+
+    def greet(self, col_too):
+        barrier = pltpu.get_barrier_semaphore()
+        others = [{"row": self.row(self.z_at(d), self.x)} for d in range(1, self.deep)]
+        others += [{"row": self.row(self.z, self.x_at(e))} for e in range(1, self.across)]
+        if col_too:
+            others.append({"col": 1 - lax.axis_index("col")})
+        for other in others:
+            pl.semaphore_signal(barrier, inc=1, device_id=other, device_id_type=MESH)
+        pl.semaphore_wait(barrier, len(others))
+
+
+class Gather:
+    def __init__(self, place, own, held, z_send, z_recv, x_send, x_recv):
+        self.p, self.own, self.held = place, own, held
+        self.sems = z_send, z_recv, x_send, x_recv
+
+    def z_copy(self, d, row, src=None):
+        p = self.p
+        return pltpu.make_async_remote_copy(
+            src_ref=self.held.at[row] if src is None else src,
+            dst_ref=self.held.at[row],
+            send_sem=self.sems[0].at[d - 1],
+            recv_sem=self.sems[1].at[d - 1],
+            device_id={"row": p.row(p.z_at(d), p.x)},
+            device_id_type=MESH,
+        )
+
+    def x_copy(self, d, e, row, src=None):
+        p = self.p
+        return pltpu.make_async_remote_copy(
+            src_ref=self.held.at[row] if src is None else src,
+            dst_ref=self.held.at[row],
+            send_sem=self.sems[2].at[d, e - 1],
+            recv_sem=self.sems[3].at[d, e - 1],
+            device_id={"row": p.row(p.z, p.x_at(e))},
+            device_id_type=MESH,
+        )
+
+    def start(self):
+        p = self.p
+        for d in range(1, p.deep):
+            self.z_copy(d, p.me, self.own).start()
+        for e in range(1, p.across):
+            self.x_copy(0, e, p.me, self.own).start()
+
+    def forward(self, d):
+        p = self.p
+        row = p.row(p.z_at(-d), p.x)
+        self.z_copy(d, row).wait_recv()
+        for e in range(1, p.across):
+            self.x_copy(d, e, row).start()
+
+    def group(self, d):
+        p = self.p
+        for e in range(1, p.across):
+            self.x_copy(d, e, p.row(p.z_at(-d), p.x_at(-e))).wait_recv()
+
+    def finish(self):
+        p = self.p
+        for d in range(1, p.deep):
+            self.z_copy(d, p.me, self.own).wait_send()
+        for d in range(p.deep):
+            row = p.row(p.z_at(-d), p.x)
+            for e in range(1, p.across):
+                self.x_copy(d, e, row).wait_send()
+
+
+def gather_sems(rows):
+    deep, across = lines_of(rows)
+    dma = pltpu.SemaphoreType.DMA
+    line, cross = (deep - 1,), (deep, across - 1)
+    return [dma(line), dma(line), dma(cross), dma(cross)]
+
+
+def hidden_kernel(
+    rows, tile, cot_ref, gate_ref, up_ref, down_ref,
+    cot_out, hidden_ref, gg_ref, gu_ref,
+    down, held, part, theirs, gates, ups,
+    z_send, z_recv, x_send, x_recv, p_send, p_recv, s_send, s_recv, local,
+):
+    p = Place(rows)
+    col = lax.axis_index("col")
+    deep, half = p.deep, p.deep // 2
+    size = p.across * cot_ref.shape[0]
+    depth, ff = cot_ref.shape[1], down_ref.shape[0]
+    get_own = pltpu.make_async_copy(cot_ref, held.at[p.me], local.at[0])
+    get_down = pltpu.make_async_copy(down_ref, down, local.at[1])
+    mine = pl.ds(col * half, half)
+    get_gate = pltpu.make_async_copy(gate_ref, gates.at[mine], local.at[2])
+    get_up = pltpu.make_async_copy(up_ref, ups.at[mine], local.at[3])
+    get_own.start()
+    get_down.start()
+    get_gate.start()
+    get_up.start()
+    p.greet(True)
+
+    def saved(n, src, dst, at):
+        return pltpu.make_async_remote_copy(
+            src_ref=src, dst_ref=dst.at[pl.ds(at * half, half)],
+            send_sem=s_send.at[n], recv_sem=s_recv.at[n],
+            device_id={"col": 1 - col}, device_id_type=MESH,
+        )
+
+    def share(d):
+        return pltpu.make_async_remote_copy(
+            src_ref=part.at[d], dst_ref=theirs.at[d],
+            send_sem=p_send.at[d], recv_sem=p_recv.at[d],
+            device_id={"col": 1 - col}, device_id_type=MESH,
+        )
+
+    gather = Gather(p, cot_ref, held, z_send, z_recv, x_send, x_recv)
+    gather.start()
+    saved(0, gate_ref, gates, col).start()
+    saved(1, up_ref, ups, col).start()
+    get_own.wait()
+    get_down.wait()
+
+    def activations(d):
+        z = p.z_at(-d)
+        share(d).wait_recv()
+
+        def some(i, carry):
+            at = pl.ds(pl.multiple_of(i * 16, 16), 16)
+            outs = swiglu_back(gates[z, at, :], ups[z, at, :], part[d, at, :] + theirs[d, at, :])
+            for ref, value in zip((hidden_ref, gg_ref, gu_ref), outs):
+                ref[z, at, :] = value
+            return carry
+
+        lax.fori_loop(0, size // 16, some, 0)
+
+    for d in range(deep):
+        z = p.z_at(-d)
+        if d > 0:
+            gather.forward(d)
+        gather.group(d)
+        left = held[pl.ds(z * p.across, p.across)].reshape(size, depth)
+
+        def some(j, carry):
+            at = pl.ds(pl.multiple_of(j * tile, tile), tile)
+            part[d, :, at] = lax.dot_general(
+                left, down[at, :], COLS, preferred_element_type=jnp.float32
+            )
+            return carry
+
+        lax.fori_loop(0, ff // tile, some, 0)
+        share(d).start()
+        if d == 0:
+            get_gate.wait()
+            get_up.wait()
+            saved(0, gate_ref, gates, 1 - col).wait_recv()
+            saved(1, up_ref, ups, 1 - col).wait_recv()
+        else:
+            activations(d - 1)
+    put = pltpu.make_async_copy(held, cot_out, local.at[0])
+    put.start()
+    activations(deep - 1)
+    gather.finish()
+    saved(0, gate_ref, gates, col).wait_send()
+    saved(1, up_ref, ups, col).wait_send()
+    for d in range(deep):
+        share(d).wait_send()
+    put.wait()
+
+
+def inputs_kernel(
+    rows, tile, in_ref, gg_ref, gu_ref, gate_ref, up_ref,
+    in_out, out_ref,
+    gate, up, tot, own, to_x, from_x, to_z, from_z,
+    z_send, z_recv, x_send, x_recv, rx_send, rx_recv, rz_send, rz_recv, local,
+):
+    p = Place(rows)
+    deep, across = p.deep, p.across
+    tok, depth = in_ref.shape
+    get_gate = pltpu.make_async_copy(gate_ref, gate, local.at[0])
+    get_up = pltpu.make_async_copy(up_ref, up, local.at[1])
+    put_own = pltpu.make_async_copy(in_ref, in_out.at[p.me], local.at[2])
+    get_gate.start()
+    get_up.start()
+    put_own.start()
+    p.greet(False)
+    gather = Gather(p, in_ref, in_out, z_send, z_recv, x_send, x_recv)
+    gather.start()
+
+    def over_x(d, e):
+        return pltpu.make_async_remote_copy(
+            src_ref=to_x.at[d, e - 1], dst_ref=from_x.at[d, e - 1],
+            send_sem=rx_send.at[d, e - 1], recv_sem=rx_recv.at[d, e - 1],
+            device_id={"row": p.row(p.z, p.x_at(e))}, device_id_type=MESH,
+        )
+
+    def over_z(d):
+        return pltpu.make_async_remote_copy(
+            src_ref=to_z.at[d - 1], dst_ref=from_z.at[d - 1],
+            send_sem=rz_send.at[d - 1], recv_sem=rz_recv.at[d - 1],
+            device_id={"row": p.row(p.z_at(d), p.x)}, device_id_type=MESH,
+        )
+
+    def columns(step):
+        def some(j, carry):
+            step(pl.ds(pl.multiple_of(j * tile, tile), tile))
+            return carry
+
+        lax.fori_loop(0, depth // tile, some, 0)
+
+    def along_x(d, at):
+        total = own[d, :, at]
+        for e in range(1, across):
+            total += from_x[d, e - 1, :, at].astype(jnp.float32)
+        return total
+
+    def pass_on(d):
+        for e in range(1, across):
+            over_x(d, e).wait_recv()
+
+        def step(at):
+            to_z[d - 1, :, at] = along_x(d, at).astype(jnp.bfloat16)
+
+        columns(step)
+        over_z(d).start()
+
+    get_gate.wait()
+    get_up.wait()
+    put_own.wait()
+    order = list(range(1, deep)) + [0]
+    for n, d in enumerate(order):
+        z = p.z_at(d)
+
+        def step(at):
+            total = lax.dot_general(
+                gg_ref[z], gate[at, :], COLS, preferred_element_type=jnp.float32
+            ) + lax.dot_general(gu_ref[z], up[at, :], COLS, preferred_element_type=jnp.float32)
+            tot[...] = total.reshape(across, tok, tile)
+            own[d, :, at] = tot[p.x]
+            for e in range(1, across):
+                to_x[d, e - 1, :, at] = tot[p.x_at(e)].astype(jnp.bfloat16)
+
+        columns(step)
+        for e in range(1, across):
+            over_x(d, e).start()
+        if n > 0:
+            pass_on(order[n - 1])
+            gather.forward(n)
+    for d in range(deep):
+        gather.group(d)
+    for e in range(1, across):
+        over_x(0, e).wait_recv()
+    for d in range(1, deep):
+        over_z(d).wait_recv()
+
+    def step(at):
+        total = along_x(0, at)
+        for d in range(1, deep):
+            total += from_z[d - 1, :, at].astype(jnp.float32)
+        out_ref[:, at] = total.astype(jnp.bfloat16)
+
+    columns(step)
+    gather.finish()
+    for d in range(deep):
+        for e in range(1, across):
+            over_x(d, e).wait_send()
+    for d in range(1, deep):
+        over_z(d).wait_send()
+
+
+def per_device(inputs, gate_saved, up_saved, cotangent, gate_weight, up_weight, down_weight):
+    rows, cols = lax.axis_size("row"), lax.axis_size("col")
+    deep, across = lines_of(rows)
+    tok, depth = cotangent.shape
+    ff = down_weight.shape[0]
+    size = tok * across
+    if cols != 2 or tok % 16 or deep % 2 or across < 2 or ff % 256 or depth % 256:
+        return plain(
+            inputs, gate_saved, up_saved, cotangent, gate_weight, up_weight, down_weight
+        )
+    bf16, f32 = jnp.bfloat16, jnp.float32
+    dma, shape = pltpu.SemaphoreType.DMA, jax.ShapeDtypeStruct
+    vmem, anywhere = pl.BlockSpec(memory_space=pltpu.VMEM), pl.BlockSpec(memory_space=pl.ANY)
+    tile = 256 if ff % 512 or depth % 512 else 512
+    halves = (deep // 2, size, ff)
+    cot_all, hidden, gg, gu = pl.pallas_call(
+        functools.partial(hidden_kernel, rows, tile),
+        in_specs=[anywhere] * 4,
+        out_specs=[anywhere, vmem, vmem, vmem],
+        out_shape=[shape((rows, tok, depth), bf16)] + [shape((deep, size, ff), bf16)] * 3,
+        scratch_shapes=[
+            pltpu.VMEM((ff, depth), bf16),
+            pltpu.VMEM((rows, tok, depth), bf16),
+            pltpu.VMEM((deep, size, ff), f32),
+            pltpu.VMEM((deep, size, ff), f32),
+            pltpu.VMEM((deep, size, ff), bf16),
+            pltpu.VMEM((deep, size, ff), bf16),
+            *gather_sems(rows),
+            dma((deep,)), dma((deep,)), dma((2,)), dma((2,)), dma((4,)),
+        ],
+        cost_estimate=pl.CostEstimate(
+            flops=2 * rows * tok * depth * ff, bytes_accessed=2 * ff * depth, transcendentals=0
+        ),
+        compiler_params=pltpu.CompilerParams(
+            collective_id=0, has_side_effects=True, vmem_limit_bytes=58 * 2**20
+        ),
+    )(cotangent, gate_saved.reshape(halves), up_saved.reshape(halves), down_weight)
+    inputs_all, grad_inputs = pl.pallas_call(
+        functools.partial(inputs_kernel, rows, tile),
+        in_specs=[anywhere, vmem, vmem, anywhere, anywhere],
+        out_specs=[anywhere, vmem],
+        out_shape=[shape((rows, tok, depth), bf16), shape((tok, depth), bf16)],
+        scratch_shapes=[
+            pltpu.VMEM((depth, ff), bf16),
+            pltpu.VMEM((depth, ff), bf16),
+            pltpu.VMEM((across, tok, tile), f32),
+            pltpu.VMEM((deep, tok, depth), f32),
+            pltpu.VMEM((deep, across - 1, tok, depth), bf16),
+            pltpu.VMEM((deep, across - 1, tok, depth), bf16),
+            pltpu.VMEM((deep - 1, tok, depth), bf16),
+            pltpu.VMEM((deep - 1, tok, depth), bf16),
+            *gather_sems(rows),
+            *gather_sems(rows)[2:],
+            *gather_sems(rows)[:2],
+            dma((3,)),
+        ],
+        cost_estimate=pl.CostEstimate(
+            flops=4 * rows * tok * depth * ff, bytes_accessed=4 * ff * depth, transcendentals=0
+        ),
+        compiler_params=pltpu.CompilerParams(
+            collective_id=1, has_side_effects=True, vmem_limit_bytes=58 * 2**20
+        ),
+    )(inputs, gg, gu, gate_weight, up_weight)
+    flat = lambda a: a.reshape(-1, a.shape[-1])
+    (grad_down,) = weight_grads(flat(hidden), (flat(cot_all),), max(1, ff // 256))
+    grad_gate, grad_up = weight_grads(flat(inputs_all), (flat(gg), flat(gu)), 8)
+    return (grad_inputs, grad_gate, grad_up, grad_down)
+
+
 def solution(mesh):
     return jax.shard_map(
         per_device,

time: 380 us -> 246 us (0.65)
  waiting for transfers between devices: 271 us -> 0 us
  Pallas kernels: 37 us -> 245 us
  matrix products: 46.7 us -> 0 us
  between operations: 14.1 us -> 0.65 us
  other arithmetic: 7.73 us -> 0 us
    pallas_call x0 -> x2, Pallas kernels: none -> 208 us  [the longest x1 114 us: per_device(): pl.pallas_call(functools.partial(inputs_kernel, rows, tile), in_specs=[an...]
    reduce_scatter x1 -> x0, waiting for transfers between devices: 129 us -> none  [per_device(): lax.psum_scatter(total, 'row', scatter_dimension=0, tiled=True)]
    all_gather x4 -> x0, waiting for transfers between devices: 107 us -> none  [the longest x1 74 us: per_device(): cotan_all = lax.all_gather(cotangent, 'row', axis=0, tiled=True)]
    dot_general x3 -> x0, matrix products: 46.7 us -> none  [the longest x1 16 us: per_device(): lax.dot_general(grad_g, gate_weight, COLS, preferred_element_type=jnp.flo...]
    psum x1 -> x0, waiting for transfers between devices: 32.5 us -> none  [per_device(): summed = lax.psum(partial_hidden, 'col')]
    convert_element_type x2 -> x0, other arithmetic: 7.73 us -> none  [the longest x1 5.66 us: swiglu_back(): grad_up_act = (grad_hidden * gvals * sigma).astype(jnp.bfloat16)]
  transfers between devices with their start and end apart: 6 -> 0, of which waited for: 5 -> 0; matrix products, arithmetic and copies ran while one was open for 14% -> 0% of each run, Pallas kernels for 10% -> 0%
where the time goes in v2:
time: 246 us
  Pallas kernels  245 us (100%)
    pallas_call x1, Pallas kernels, per_device(): pl.pallas_call(functools.partial(inputs_kernel, rows, tile), in_specs=[an...  114 us
    pallas_call x1, Pallas kernels, per_device(): pl.pallas_call(functools.partial(hidden_kernel, rows, tile), in_specs=[an...  93.3 us
    pallas_call x2, Pallas kernels, weight_grads(): pl.pallas_call(kern, grid=(blocks,), in_specs=[pl.BlockSpec((tokens, bm),...  36.9 us

profile of v2, /device:TPU:17, one launch (start us, length us, event | category | flops | bytes accessed | tf_op | source)
XLA Modules:
  0.0 246.0 jit_solution(16244690087614010607)
XLA Ops:
  0.6 93.3 %shard_map.102 = (bf16[8,64,4096]{2,1,0:T(8,128)(2,1)}, bf16[4,128,2048]{2,1,0:T(8,128)(2,1)}, bf16[4,128,2048]{2,1,0:T(8,128)(2,1)}, bf16[4,128,2048]{2,1,0:T(8,128)(2,1)}) custom-call(bf16[64,4096]{1,0:T(8,128)(2,1)} %cot_ref.1, bf16[2,128,2048]{2,1,0:T(8,128)(2,1)} %bitcast.7, bf16[2,128,2048]{2,1,0:T(8,128)(2,1)} %bitcast.8, bf16[2048,4096]{1,0:T(8,128)(2,1)} %down_ref.1), custom_call_target="tpu_custom_call" | custom-call | flops 8589934592 | bytes 16777216 | tf_op jit(solution)/shard_map/pallas_call | solution.py:381
  93.9 114.3 %shard_map.103 = (bf16[8,64,4096]{2,1,0:T(8,128)(2,1)}, bf16[64,4096]{1,0:T(8,128)(2,1)}) custom-call(bf16[64,4096]{1,0:T(8,128)(2,1)} %in_ref.1, bf16[4,128,2048]{2,1,0:T(8,128)(2,1)} %get-tuple-element.12.gg_ref, bf16[4,128,2048]{2,1,0:T(8,128)(2,1)} %get-tuple-element.13.gu_ref, bf16[4096,2048]{1,0:T(8,128)(2,1)} %gate_ref.1, bf16[4096,2048]{1,0:T(8,128)(2,1)} %up_ref.1), custom_call_target="tpu_custom_call" | custom-call | flops 17179869184 | bytes 33554432 | tf_op jit(solution)/shard_map/pallas_call | solution.py:403
  208.3 22.9 %shard_map.104 = (bf16[4096,2048]{1,0:T(8,128)(2,1)}, bf16[4096,2048]{1,0:T(8,128)(2,1)}) custom-call(bf16[512,4096]{1,0:T(8,128)(2,1)} %bitcast.10, bf16[512,2048]{1,0:T(8,128)(2,1)} %bitcast.12, bf16[512,2048]{1,0:T(8,128)(2,1)} %bitcast.13), custom_call_target="tpu_custom_call" | custom-call | flops 17179869184 | bytes 41943040 | tf_op jit(solution)/shard_map/pallas_call | solution.py:39
  231.2 0.0 copy-start
  231.2 14.0 %shard_map.105 = bf16[2048,4096]{1,0:T(8,128)(2,1)} custom-call(bf16[512,2048]{1,0:T(8,128)(2,1)} %bitcast.11, bf16[512,4096]{1,0:T(8,128)(2,1)} %bitcast.9), custom_call_target="tpu_custom_call" | custom-call | flops 8589934592 | bytes 23068672 | tf_op jit(solution)/shard_map/pallas_call | solution.py:39
  245.2 0.0 copy-done
  245.2 0.8 copy.12
Async XLA Ops:
  231.2 14.0 %copy-start = (bf16[64,4096]{1,0:T(8,128)(2,1)S(1)}, bf16[64,4096]{1,0:T(8,128)(2,1)}, u32[]{:S(2)}) copy-start(bf16[64,4096]{1,0:T(8,128)(2,1)} %get-tuple-element.24) | copy-start | bytes 1572868

commit v3 on v2

--- a/solution.py
+++ b/solution.py
@@ -141,26 +141,34 @@
         p = self.p
         for d in range(1, p.deep):
             self.z_copy(d, p.me, self.own).start()
+        self.own_over_x()
+
+    def own_over_x(self):
+        for e in range(1, self.p.across):
+            self.x_copy(0, e, self.p.me, self.own).start()
+
+    def over_x(self, d):
+        p = self.p
         for e in range(1, p.across):
-            self.x_copy(0, e, p.me, self.own).start()
+            self.x_copy(d, e, p.row(p.z_at(-d), p.x)).start()
+
+    def arrived(self, d):
+        self.z_copy(d, self.p.row(self.p.z_at(-d), self.p.x)).wait_recv()
 
     def forward(self, d):
-        p = self.p
-        row = p.row(p.z_at(-d), p.x)
-        self.z_copy(d, row).wait_recv()
-        for e in range(1, p.across):
-            self.x_copy(d, e, row).start()
+        self.arrived(d)
+        self.over_x(d)
 
     def group(self, d):
         p = self.p
         for e in range(1, p.across):
             self.x_copy(d, e, p.row(p.z_at(-d), p.x_at(-e))).wait_recv()
 
-    def finish(self):
-        p = self.p
-        for d in range(1, p.deep):
+    def finish(self, over_z, over_x):
+        p = self.p
+        for d in over_z:
             self.z_copy(d, p.me, self.own).wait_send()
-        for d in range(p.deep):
+        for d in over_x:
             row = p.row(p.z_at(-d), p.x)
             for e in range(1, p.across):
                 self.x_copy(d, e, row).wait_send()
@@ -174,12 +182,14 @@
 
 
 def hidden_kernel(
-    rows, tile, cot_ref, gate_ref, up_ref, down_ref,
-    cot_out, hidden_ref, gg_ref, gu_ref,
+    rows, tile, cot_ref, in_ref, gate_ref, up_ref, down_ref,
+    cot_out, in_out, hidden_ref, gg_ref, gu_ref,
     down, held, part, theirs, gates, ups,
-    z_send, z_recv, x_send, x_recv, p_send, p_recv, s_send, s_recv, local,
+    z_send, z_recv, x_send, x_recv, iz_send, iz_recv, ix_send, ix_recv,
+    p_send, p_recv, s_send, s_recv, local,
 ):
     p = Place(rows)
+    early = p.deep // 2
     col = lax.axis_index("col")
     deep, half = p.deep, p.deep // 2
     size = p.across * cot_ref.shape[0]
@@ -189,8 +199,10 @@
     mine = pl.ds(col * half, half)
     get_gate = pltpu.make_async_copy(gate_ref, gates.at[mine], local.at[2])
     get_up = pltpu.make_async_copy(up_ref, ups.at[mine], local.at[3])
+    put_own = pltpu.make_async_copy(in_ref, in_out.at[p.me], local.at[4])
     get_own.start()
     get_down.start()
+    put_own.start()
     get_gate.start()
     get_up.start()
     p.greet(True)
@@ -210,6 +222,7 @@
         )
 
     gather = Gather(p, cot_ref, held, z_send, z_recv, x_send, x_recv)
+    ins = Gather(p, in_ref, in_out, iz_send, iz_recv, ix_send, ix_recv)
     gather.start()
     saved(0, gate_ref, gates, col).start()
     saved(1, up_ref, ups, col).start()
@@ -231,9 +244,15 @@
 
     for d in range(deep):
         z = p.z_at(-d)
-        if d > 0:
-            gather.forward(d)
+        if d + 1 < deep:
+            gather.forward(d + 1)
+            ins.z_copy(d + 1, p.me, in_ref).start()
+        if d + 2 == deep:
+            ins.own_over_x()
         gather.group(d)
+        if d + 1 == deep:
+            for n in range(1, early):
+                ins.forward(n)
         left = held[pl.ds(z * p.across, p.across)].reshape(size, depth)
 
         def some(j, carry):
@@ -255,7 +274,13 @@
     put = pltpu.make_async_copy(held, cot_out, local.at[0])
     put.start()
     activations(deep - 1)
-    gather.finish()
+    for d in range(early, deep):
+        ins.arrived(d)
+    for d in range(early):
+        ins.group(d)
+    gather.finish(range(1, deep), range(deep))
+    ins.finish(range(1, deep), range(early))
+    put_own.wait()
     saved(0, gate_ref, gates, col).wait_send()
     saved(1, up_ref, ups, col).wait_send()
     for d in range(deep):
@@ -267,20 +292,27 @@
     rows, tile, in_ref, gg_ref, gu_ref, gate_ref, up_ref,
     in_out, out_ref,
     gate, up, tot, own, to_x, from_x, to_z, from_z,
-    z_send, z_recv, x_send, x_recv, rx_send, rx_recv, rz_send, rz_recv, local,
+    x_send, x_recv, rx_send, rx_recv, rz_send, rz_recv, local,
 ):
     p = Place(rows)
     deep, across = p.deep, p.across
-    tok, depth = in_ref.shape
-    get_gate = pltpu.make_async_copy(gate_ref, gate, local.at[0])
-    get_up = pltpu.make_async_copy(up_ref, up, local.at[1])
-    put_own = pltpu.make_async_copy(in_ref, in_out.at[p.me], local.at[2])
-    get_gate.start()
-    get_up.start()
-    put_own.start()
+    late = range(deep // 2, deep)
+    tok, depth = out_ref.shape
+
+    def weights(j):
+        at = pl.ds(pl.multiple_of(j * tile, tile), tile)
+        return [
+            pltpu.make_async_copy(ref.at[at, :], to.at[at, :], local.at[n, j])
+            for n, (ref, to) in enumerate(((gate_ref, gate), (up_ref, up)))
+        ]
+
+    for j in range(depth // tile):
+        for copy in weights(j):
+            copy.start()
     p.greet(False)
-    gather = Gather(p, in_ref, in_out, z_send, z_recv, x_send, x_recv)
-    gather.start()
+    gather = Gather(p, None, in_out, None, None, x_send, x_recv)
+    for d in late:
+        gather.over_x(d)
 
     def over_x(d, e):
         return pltpu.make_async_remote_copy(
@@ -298,7 +330,7 @@
 
     def columns(step):
         def some(j, carry):
-            step(pl.ds(pl.multiple_of(j * tile, tile), tile))
+            step(j, pl.ds(pl.multiple_of(j * tile, tile), tile))
             return carry
 
         lax.fori_loop(0, depth // tile, some, 0)
@@ -313,20 +345,20 @@
         for e in range(1, across):
             over_x(d, e).wait_recv()
 
-        def step(at):
+        def step(j, at):
             to_z[d - 1, :, at] = along_x(d, at).astype(jnp.bfloat16)
 
         columns(step)
         over_z(d).start()
 
-    get_gate.wait()
-    get_up.wait()
-    put_own.wait()
     order = list(range(1, deep)) + [0]
     for n, d in enumerate(order):
         z = p.z_at(d)
 
-        def step(at):
+        def step(j, at):
+            if n == 0:
+                for copy in weights(j):
+                    copy.wait()
             total = lax.dot_general(
                 gg_ref[z], gate[at, :], COLS, preferred_element_type=jnp.float32
             ) + lax.dot_general(gu_ref[z], up[at, :], COLS, preferred_element_type=jnp.float32)
@@ -338,24 +370,23 @@
         columns(step)
         for e in range(1, across):
             over_x(d, e).start()
-        if n > 0:
-            pass_on(order[n - 1])
-            gather.forward(n)
-    for d in range(deep):
-        gather.group(d)
+    for d in range(1, deep):
+        pass_on(d)
     for e in range(1, across):
         over_x(0, e).wait_recv()
     for d in range(1, deep):
         over_z(d).wait_recv()
 
-    def step(at):
+    def step(j, at):
         total = along_x(0, at)
         for d in range(1, deep):
             total += from_z[d - 1, :, at].astype(jnp.float32)
         out_ref[:, at] = total.astype(jnp.bfloat16)
 
     columns(step)
-    gather.finish()
+    for d in late:
+        gather.group(d)
+    gather.finish((), late)
     for d in range(deep):
         for e in range(1, across):
             over_x(d, e).wait_send()
@@ -378,11 +409,11 @@
     vmem, anywhere = pl.BlockSpec(memory_space=pltpu.VMEM), pl.BlockSpec(memory_space=pl.ANY)
     tile = 256 if ff % 512 or depth % 512 else 512
     halves = (deep // 2, size, ff)
-    cot_all, hidden, gg, gu = pl.pallas_call(
+    cot_all, inputs_some, hidden, gg, gu = pl.pallas_call(
         functools.partial(hidden_kernel, rows, tile),
-        in_specs=[anywhere] * 4,
-        out_specs=[anywhere, vmem, vmem, vmem],
-        out_shape=[shape((rows, tok, depth), bf16)] + [shape((deep, size, ff), bf16)] * 3,
+        in_specs=[anywhere] * 5,
+        out_specs=[anywhere, anywhere, vmem, vmem, vmem],
+        out_shape=[shape((rows, tok, depth), bf16)] * 2 + [shape((deep, size, ff), bf16)] * 3,
         scratch_shapes=[
             pltpu.VMEM((ff, depth), bf16),
             pltpu.VMEM((rows, tok, depth), bf16),
@@ -391,7 +422,8 @@
             pltpu.VMEM((deep, size, ff), bf16),
             pltpu.VMEM((deep, size, ff), bf16),
             *gather_sems(rows),
-            dma((deep,)), dma((deep,)), dma((2,)), dma((2,)), dma((4,)),
+            *gather_sems(rows),
+            dma((deep,)), dma((deep,)), dma((2,)), dma((2,)), dma((5,)),
         ],
         cost_estimate=pl.CostEstimate(
             flops=2 * rows * tok * depth * ff, bytes_accessed=2 * ff * depth, transcendentals=0
@@ -399,7 +431,7 @@
         compiler_params=pltpu.CompilerParams(
             collective_id=0, has_side_effects=True, vmem_limit_bytes=58 * 2**20
         ),
-    )(cotangent, gate_saved.reshape(halves), up_saved.reshape(halves), down_weight)
+    )(cotangent, inputs, gate_saved.reshape(halves), up_saved.reshape(halves), down_weight)
     inputs_all, grad_inputs = pl.pallas_call(
         functools.partial(inputs_kernel, rows, tile),
         in_specs=[anywhere, vmem, vmem, anywhere, anywhere],
@@ -414,18 +446,19 @@
             pltpu.VMEM((deep, across - 1, tok, depth), bf16),
             pltpu.VMEM((deep - 1, tok, depth), bf16),
             pltpu.VMEM((deep - 1, tok, depth), bf16),
-            *gather_sems(rows),
+            *gather_sems(rows)[2:],
             *gather_sems(rows)[2:],
             *gather_sems(rows)[:2],
-            dma((3,)),
+            dma((2, depth // tile)),
         ],
+        input_output_aliases={0: 0},
         cost_estimate=pl.CostEstimate(
             flops=4 * rows * tok * depth * ff, bytes_accessed=4 * ff * depth, transcendentals=0
         ),
         compiler_params=pltpu.CompilerParams(
             collective_id=1, has_side_effects=True, vmem_limit_bytes=58 * 2**20
         ),
-    )(inputs, gg, gu, gate_weight, up_weight)
+    )(inputs_some, gg, gu, gate_weight, up_weight)
     flat = lambda a: a.reshape(-1, a.shape[-1])
     (grad_down,) = weight_grads(flat(hidden), (flat(cot_all),), max(1, ff // 256))
     grad_gate, grad_up = weight_grads(flat(inputs_all), (flat(gg), flat(gu)), 8)

time: 246 us -> 244 us (level); the launches traced: 246 us -> 240 us
  Pallas kernels: 245 us -> 239 us
    pallas_call x1, Pallas kernels: 114 us -> 106 us  [per_device(): pl.pallas_call(functools.partial(inputs_kernel, rows, tile), in_specs=[an...]
    pallas_call x1, Pallas kernels: 93.3 us -> 96.2 us  [per_device(): pl.pallas_call(functools.partial(hidden_kernel, rows, tile), in_specs=[an...]
where the time goes in v3:
time: 244 us; the launch traced here: 240 us
  Pallas kernels  239 us (98%)
    pallas_call x1, Pallas kernels, per_device(): pl.pallas_call(functools.partial(inputs_kernel, rows, tile), in_specs=[an...  106 us
    pallas_call x1, Pallas kernels, per_device(): pl.pallas_call(functools.partial(hidden_kernel, rows, tile), in_specs=[an...  96.2 us
    pallas_call x2, Pallas kernels, weight_grads(): pl.pallas_call(kern, grid=(blocks,), in_specs=[pl.BlockSpec((tokens, bm),...  37 us

profile of v3, /device:TPU:17, one launch (start us, length us, event | category | flops | bytes accessed | tf_op | source)
XLA Modules:
  0.0 240.2 jit_solution(10745295033829201176)
XLA Ops:
  0.6 96.2 %shard_map.102 = (bf16[8,64,4096]{2,1,0:T(8,128)(2,1)}, bf16[8,64,4096]{2,1,0:T(8,128)(2,1)}, bf16[4,128,2048]{2,1,0:T(8,128)(2,1)}, bf16[4,128,2048]{2,1,0:T(8,128)(2,1)}, bf16[4,128,2048]{2,1,0:T(8,128)(2,1)}) custom-call(bf16[64,4096]{1,0:T(8,128)(2,1)} %cot_ref.1, bf16[64,4096]{1,0:T(8,128)(2,1)} %in_ref.1, bf16[2,128,2048]{2,1,0:T(8,128)(2,1)} %bitcast.7, ...), custom_call_target="tpu_custom_call" | custom-call | flops 8589934592 | bytes 16777216 | tf_op jit(solution)/shard_map/pallas_call | solution.py:412
  96.9 105.6 %shard_map.103 = (bf16[8,64,4096]{2,1,0:T(8,128)(2,1)}, bf16[64,4096]{1,0:T(8,128)(2,1)}) custom-call(bf16[8,64,4096]{2,1,0:T(8,128)(2,1)} %get-tuple-element.13.in_ref, bf16[4,128,2048]{2,1,0:T(8,128)(2,1)} %get-tuple-element.14.gg_ref, bf16[4,128,2048]{2,1,0:T(8,128)(2,1)} %get-tuple-element.15.gu_ref, ...), custom_call_target="tpu_custom_call", output_to_operand_aliasing={{0}: (0, {})} | custom-call | flops 17179869184 | bytes 33554432 | tf_op jit(solution)/shard_map/pallas_call | solution.py:435
  202.5 22.9 %shard_map.104 = (bf16[4096,2048]{1,0:T(8,128)(2,1)}, bf16[4096,2048]{1,0:T(8,128)(2,1)}) custom-call(bf16[512,4096]{1,0:T(8,128)(2,1)} %bitcast.10, bf16[512,2048]{1,0:T(8,128)(2,1)} %bitcast.12, bf16[512,2048]{1,0:T(8,128)(2,1)} %bitcast.13), custom_call_target="tpu_custom_call" | custom-call | flops 17179869184 | bytes 41943040 | tf_op jit(solution)/shard_map/pallas_call | solution.py:39
  225.4 0.0 copy-start
  225.4 14.0 %shard_map.105 = bf16[2048,4096]{1,0:T(8,128)(2,1)} custom-call(bf16[512,2048]{1,0:T(8,128)(2,1)} %bitcast.11, bf16[512,4096]{1,0:T(8,128)(2,1)} %bitcast.9), custom_call_target="tpu_custom_call" | custom-call | flops 8589934592 | bytes 23068672 | tf_op jit(solution)/shard_map/pallas_call | solution.py:39
  239.4 0.0 copy-done
  239.4 0.8 copy.14
Async XLA Ops:
  225.4 14.0 %copy-start = (bf16[64,4096]{1,0:T(8,128)(2,1)S(1)}, bf16[64,4096]{1,0:T(8,128)(2,1)}, u32[]{:S(2)}) copy-start(bf16[64,4096]{1,0:T(8,128)(2,1)} %get-tuple-element.26) | copy-start | bytes 1572868

commit v4 on v3

--- a/solution.py
+++ b/solution.py
@@ -84,6 +84,10 @@
     return rows // across, across
 
 
+def steps_of(deep):
+    return [0, 1] + ([deep - 1] if deep > 2 else []) + list(range(2, deep - 1))
+
+
 class Place:
     def __init__(self, rows):
         self.deep, self.across = lines_of(rows)
@@ -137,11 +141,8 @@
             device_id_type=MESH,
         )
 
-    def start(self):
-        p = self.p
-        for d in range(1, p.deep):
-            self.z_copy(d, p.me, self.own).start()
-        self.own_over_x()
+    def along_z(self, d):
+        self.z_copy(d, self.p.me, self.own).start()
 
     def own_over_x(self):
         for e in range(1, self.p.across):
@@ -154,10 +155,6 @@
 
     def arrived(self, d):
         self.z_copy(d, self.p.row(self.p.z_at(-d), self.p.x)).wait_recv()
-
-    def forward(self, d):
-        self.arrived(d)
-        self.over_x(d)
 
     def group(self, d):
         p = self.p
@@ -189,6 +186,7 @@
     p_send, p_recv, s_send, s_recv, local,
 ):
     p = Place(rows)
+    steps = steps_of(p.deep)
     early = p.deep // 2
     col = lax.axis_index("col")
     deep, half = p.deep, p.deep // 2
@@ -223,7 +221,8 @@
 
     gather = Gather(p, cot_ref, held, z_send, z_recv, x_send, x_recv)
     ins = Gather(p, in_ref, in_out, iz_send, iz_recv, ix_send, ix_recv)
-    gather.start()
+    gather.along_z(steps[1])
+    gather.own_over_x()
     saved(0, gate_ref, gates, col).start()
     saved(1, up_ref, ups, col).start()
     get_own.wait()
@@ -242,17 +241,27 @@
 
         lax.fori_loop(0, size // 16, some, 0)
 
-    for d in range(deep):
+    for k, d in enumerate(steps):
         z = p.z_at(-d)
-        if d + 1 < deep:
-            gather.forward(d + 1)
-            ins.z_copy(d + 1, p.me, in_ref).start()
-        if d + 2 == deep:
-            ins.own_over_x()
+        if k + 1 < deep:
+            gather.arrived(steps[k + 1])
+            if k + 2 < deep:
+                gather.along_z(steps[k + 2])
+            else:
+                ins.along_z(steps[1])
+            gather.over_x(steps[k + 1])
+            if k + 3 == deep:
+                ins.own_over_x()
+        else:
+            for n in range(1, deep - 1):
+                ins.arrived(steps[n])
+                if n + 1 < deep - 1:
+                    ins.along_z(steps[n + 1])
+                if n < early:
+                    ins.over_x(steps[n])
+                if n + 1 == early:
+                    break
         gather.group(d)
-        if d + 1 == deep:
-            for n in range(1, early):
-                ins.forward(n)
         left = held[pl.ds(z * p.across, p.across)].reshape(size, depth)
 
         def some(j, carry):
@@ -264,22 +273,24 @@
 
         lax.fori_loop(0, ff // tile, some, 0)
         share(d).start()
-        if d == 0:
+        if k == 0:
             get_gate.wait()
             get_up.wait()
             saved(0, gate_ref, gates, 1 - col).wait_recv()
             saved(1, up_ref, ups, 1 - col).wait_recv()
         else:
-            activations(d - 1)
+            activations(steps[k - 1])
     put = pltpu.make_async_copy(held, cot_out, local.at[0])
     put.start()
-    activations(deep - 1)
-    for d in range(early, deep):
-        ins.arrived(d)
-    for d in range(early):
+    activations(steps[-1])
+    for n in range(early, deep - 1):
+        ins.arrived(steps[n])
+        if n + 1 < deep - 1:
+            ins.along_z(steps[n + 1])
+    for d in steps[:early]:
         ins.group(d)
     gather.finish(range(1, deep), range(deep))
-    ins.finish(range(1, deep), range(early))
+    ins.finish(steps[1:-1], steps[:early])
     put_own.wait()
     saved(0, gate_ref, gates, col).wait_send()
     saved(1, up_ref, ups, col).wait_send()
@@ -289,14 +300,15 @@
 
 
 def inputs_kernel(
-    rows, tile, in_ref, gg_ref, gu_ref, gate_ref, up_ref,
+    rows, tile, some_ref, gg_ref, gu_ref, gate_ref, up_ref,
     in_out, out_ref,
     gate, up, tot, own, to_x, from_x, to_z, from_z,
-    x_send, x_recv, rx_send, rx_recv, rz_send, rz_recv, local,
+    z_send, z_recv, x_send, x_recv, rx_send, rx_recv, rz_send, rz_recv, local,
 ):
     p = Place(rows)
     deep, across = p.deep, p.across
-    late = range(deep // 2, deep)
+    steps = steps_of(deep)
+    late = steps[deep // 2:]
     tok, depth = out_ref.shape
 
     def weights(j):
@@ -310,9 +322,10 @@
         for copy in weights(j):
             copy.start()
     p.greet(False)
-    gather = Gather(p, None, in_out, None, None, x_send, x_recv)
-    for d in late:
+    gather = Gather(p, in_out.at[p.me], in_out, z_send, z_recv, x_send, x_recv)
+    for d in late[:-1]:
         gather.over_x(d)
+    gather.along_z(late[-1])
 
     def over_x(d, e):
         return pltpu.make_async_remote_copy(
@@ -351,7 +364,7 @@
         columns(step)
         over_z(d).start()
 
-    order = list(range(1, deep)) + [0]
+    order = steps[:0:-1] + [0]
     for n, d in enumerate(order):
         z = p.z_at(d)
 
@@ -370,8 +383,11 @@
         columns(step)
         for e in range(1, across):
             over_x(d, e).start()
-    for d in range(1, deep):
-        pass_on(d)
+        if n > 1:
+            pass_on(order[n - 2])
+    gather.arrived(late[-1])
+    gather.over_x(late[-1])
+    pass_on(order[deep - 2])
     for e in range(1, across):
         over_x(0, e).wait_recv()
     for d in range(1, deep):
@@ -386,7 +402,7 @@
     columns(step)
     for d in late:
         gather.group(d)
-    gather.finish((), late)
+    gather.finish(late[-1:], late)
     for d in range(deep):
         for e in range(1, across):
             over_x(d, e).wait_send()
@@ -400,7 +416,7 @@
     tok, depth = cotangent.shape
     ff = down_weight.shape[0]
     size = tok * across
-    if cols != 2 or tok % 16 or deep % 2 or across < 2 or ff % 256 or depth % 256:
+    if cols != 2 or tok % 16 or deep % 2 or deep < 4 or across < 2 or ff % 256 or depth % 256:
         return plain(
             inputs, gate_saved, up_saved, cotangent, gate_weight, up_weight, down_weight
         )
@@ -446,7 +462,7 @@
             pltpu.VMEM((deep, across - 1, tok, depth), bf16),
             pltpu.VMEM((deep - 1, tok, depth), bf16),
             pltpu.VMEM((deep - 1, tok, depth), bf16),
-            *gather_sems(rows)[2:],
+            *gather_sems(rows),
             *gather_sems(rows)[2:],
             *gather_sems(rows)[:2],
             dma((2, depth // tile)),

time: 244 us -> 210 us (0.86)
  Pallas kernels: 239 us -> 206 us
    pallas_call x1, Pallas kernels: 96.2 us -> 79 us  [per_device(): pl.pallas_call(functools.partial(hidden_kernel, rows, tile), in_specs=[an...]
    pallas_call x1, Pallas kernels: 106 us -> 90 us  [per_device(): pl.pallas_call(functools.partial(inputs_kernel, rows, tile), in_specs=[an...]
where the time goes in v4:
time: 210 us; the launch traced here: 207 us
  Pallas kernels  206 us (98%)
    pallas_call x1, Pallas kernels, per_device(): pl.pallas_call(functools.partial(inputs_kernel, rows, tile), in_specs=[an...  90 us
    pallas_call x1, Pallas kernels, per_device(): pl.pallas_call(functools.partial(hidden_kernel, rows, tile), in_specs=[an...  79 us
    pallas_call x2, Pallas kernels, weight_grads(): pl.pallas_call(kern, grid=(blocks,), in_specs=[pl.BlockSpec((tokens, bm),...  36.9 us

profile of v4, /device:TPU:17, one launch (start us, length us, event | category | flops | bytes accessed | tf_op | source)
XLA Modules:
  0.0 207.4 jit_solution(17462274840709348385)
XLA Ops:
  0.6 79.0 %shard_map.102 = (bf16[8,64,4096]{2,1,0:T(8,128)(2,1)}, bf16[8,64,4096]{2,1,0:T(8,128)(2,1)}, bf16[4,128,2048]{2,1,0:T(8,128)(2,1)}, bf16[4,128,2048]{2,1,0:T(8,128)(2,1)}, bf16[4,128,2048]{2,1,0:T(8,128)(2,1)}) custom-call(bf16[64,4096]{1,0:T(8,128)(2,1)} %cot_ref.1, bf16[64,4096]{1,0:T(8,128)(2,1)} %in_ref.1, bf16[2,128,2048]{2,1,0:T(8,128)(2,1)} %bitcast.7, ...), custom_call_target="tpu_custom_call" | custom-call | flops 8589934592 | bytes 16777216 | tf_op jit(solution)/shard_map/pallas_call | solution.py:428
  79.7 90.0 %shard_map.103 = (bf16[8,64,4096]{2,1,0:T(8,128)(2,1)}, bf16[64,4096]{1,0:T(8,128)(2,1)}) custom-call(bf16[8,64,4096]{2,1,0:T(8,128)(2,1)} %get-tuple-element.13.some_ref, bf16[4,128,2048]{2,1,0:T(8,128)(2,1)} %get-tuple-element.14.gg_ref, bf16[4,128,2048]{2,1,0:T(8,128)(2,1)} %get-tuple-element.15.gu_ref, ...), custom_call_target="tpu_custom_call", output_to_operand_aliasing={{0}: (0, {})} | custom-call | flops 17179869184 | bytes 33554432 | tf_op jit(solution)/shard_map/pallas_call | solution.py:451
  169.7 22.9 %shard_map.104 = (bf16[4096,2048]{1,0:T(8,128)(2,1)}, bf16[4096,2048]{1,0:T(8,128)(2,1)}) custom-call(bf16[512,4096]{1,0:T(8,128)(2,1)} %bitcast.10, bf16[512,2048]{1,0:T(8,128)(2,1)} %bitcast.12, bf16[512,2048]{1,0:T(8,128)(2,1)} %bitcast.13), custom_call_target="tpu_custom_call" | custom-call | flops 17179869184 | bytes 41943040 | tf_op jit(solution)/shard_map/pallas_call | solution.py:39
  192.6 0.0 copy-start
  192.6 14.0 %shard_map.105 = bf16[2048,4096]{1,0:T(8,128)(2,1)} custom-call(bf16[512,2048]{1,0:T(8,128)(2,1)} %bitcast.11, bf16[512,4096]{1,0:T(8,128)(2,1)} %bitcast.9), custom_call_target="tpu_custom_call" | custom-call | flops 8589934592 | bytes 23068672 | tf_op jit(solution)/shard_map/pallas_call | solution.py:39
  206.6 0.0 copy-done
  206.6 0.8 copy.14
Async XLA Ops:
  192.6 14.0 %copy-start = (bf16[64,4096]{1,0:T(8,128)(2,1)S(1)}, bf16[64,4096]{1,0:T(8,128)(2,1)}, u32[]{:S(2)}) copy-start(bf16[64,4096]{1,0:T(8,128)(2,1)} %get-tuple-element.26) | copy-start | bytes 1572868
